TPU v7x, 32 devices: a whole 2x2x4 slice. The times are simulated.
32 devices in a mesh: groups: 2 (over x), dap: 16 (over z, y, core).
Axes of the slice: x: 2, y: 2, z: 4, core: 2. Of those that a mesh axis runs over, the one named last changes fastest.
Arguments:
- pair_act: bfloat16 [64, 32, 128], P(('groups', 'dap')), parts along dimension 0, may hold values from -3 to 3
- chain_id: int32 [64], P('groups'), parts along dimension 0, may hold values from 0 to 3, as said below
- pad_mask: int32 [64], P('groups'), parts along dimension 0, may hold values from 0 to 1, as said below
- chain_table: float32 [2, 128], replicated, may hold values from -3 to 3
- out_project: bfloat16 [128, 512], replicated, may hold values from -0.5 to 0.5
- out_gate: bfloat16 [128, 128], replicated, may hold values from -0.5 to 0.5
- out_final: bfloat16 [128, 128], replicated, may hold values from -0.5 to 0.5
- in_project: bfloat16 [128, 512], replicated, may hold values from -0.5 to 0.5
- in_gate: bfloat16 [128, 128], replicated, may hold values from -0.5 to 0.5
- in_final: bfloat16 [128, 128], replicated, may hold values from -1 to 1
- start_project: bfloat16 [128, 512], replicated, may hold values from -0.5 to 0.5
- start_bias: bfloat16 [128, 4], replicated, may hold values from -1.75 to 1.75
- start_final: bfloat16 [128, 128], replicated, may hold values from -1.5 to 1.5
- end_project: bfloat16 [128, 512], replicated, may hold values from -0.5 to 0.5
- end_bias: bfloat16 [128, 4], replicated, may hold values from -1.75 to 1.75
- end_final: bfloat16 [128, 128], replicated, may hold values from -1.5 to 1.5
- trans_up: bfloat16 [128, 512], replicated, may hold values from -0.5 to 0.5
- trans_down: bfloat16 [512, 128], replicated, may hold values from -0.25 to 0.25
Outputs:
- pair_out: bfloat16 [64, 32, 128], P(('groups', 'dap')), parts along dimension 0
There are 2 independent parts, one for each index of `groups`. A program takes and returns all parts, laid end to end along the dimension named above; an argument that names none is the same for every part. Nothing has to cross between parts.
Inputs may be any that keep to these rules, and one draw needn't show every extreme that they name: `chain_id`: chain numbers never fall along the residues; the first residue is in chain 0 and the last in chain 3. `pad_mask`: real residues (1) come first, padding (0) after; at least 16 residues are real and the last one is always padding.
All inputs are finite; a program needn't handle non-finite values.
Results may differ from a plain program's by a relative error of at most 0.025.
Values may be sent and summed in bfloat16 or wider, within the bound.
A program may use at most 64 MiB of HBM per device.

v0:
```python
import math

import jax
import jax.numpy as jnp
from jax import lax
from jax.sharding import PartitionSpec as P

epsilon = 1e-05
mask_scale = 1000000000.0


def layer_norm(values, along_axis):
    values = values.astype(jnp.float32)
    centred = values - jnp.mean(values, axis=along_axis, keepdims=True)
    spread = jnp.mean(centred * centred, axis=along_axis, keepdims=True)
    return centred * lax.rsqrt(spread + epsilon)


def regroup_second(values):
    return lax.all_to_all(values, "dap", split_axis=1, concat_axis=0, tiled=True)


def return_columns(values):
    return lax.all_to_all(values, "dap", split_axis=0, concat_axis=1, tiled=True)


def softmax_rows(scores):
    scores = scores - jnp.max(scores, axis=-1, keepdims=True)
    expsum = jnp.exp(scores)
    return (expsum / jnp.sum(expsum, axis=-1, keepdims=True)).astype(jnp.bfloat16)


def triangle_product(
    current, mask_rows, mask_all, weight_project, weight_gate, weight_final, outgoing
):
    hidden_width = weight_project.shape[1] // 4
    normed = layer_norm(current, -1).astype(jnp.bfloat16)
    projected = jnp.einsum(
        "ilc,ce->eil", normed, weight_project, preferred_element_type=jnp.float32
    )
    pair_mask = mask_rows[:, None] * mask_all[None, :]
    left_side = (
        pair_mask
        * jax.nn.sigmoid(projected[hidden_width : 2 * hidden_width])
        * projected[:hidden_width]
    ).astype(jnp.bfloat16)
    right_side = (
        pair_mask
        * jax.nn.sigmoid(projected[3 * hidden_width :])
        * projected[2 * hidden_width : 3 * hidden_width]
    ).astype(jnp.bfloat16)
    left_all, right_all = (
        lax.all_to_all(left_side, "dap", split_axis=0, concat_axis=1, tiled=True),
        lax.all_to_all(right_side, "dap", split_axis=0, concat_axis=1, tiled=True),
    )
    if outgoing:
        combined = jnp.einsum(
            "cik,cjk->cij", left_all, right_all, preferred_element_type=jnp.float32
        )
    else:
        combined = jnp.einsum(
            "cki,ckj->cij", left_all, right_all, preferred_element_type=jnp.float32
        )
    gathered = regroup_second(combined.astype(jnp.bfloat16))
    normed_out = layer_norm(gathered, 0).astype(jnp.bfloat16)
    update = jnp.einsum("cil,cd->ild", normed_out, weight_final, preferred_element_type=jnp.float32)
    gate_full = jax.nn.sigmoid(
        jnp.einsum("ilc,cd->ild", normed, weight_gate, preferred_element_type=jnp.float32)
    )
    return (current.astype(jnp.float32) + gate_full * update).astype(jnp.bfloat16)


def starting_node(current, mask_bias, weight_project, weight_bias, weight_final):
    row_count, length, width = current.shape
    heads = weight_bias.shape[1]
    head_dim = width // heads
    scaling = 1.0 / math.sqrt(head_dim)
    normed = layer_norm(current, -1).astype(jnp.bfloat16)
    projected = jnp.einsum(
        "ijc,ce->ije", normed, weight_project, preferred_element_type=jnp.float32
    )
    queries = (
        projected[..., :width].astype(jnp.bfloat16).reshape(row_count, length, heads, head_dim)
    )
    key_rows = (
        projected[..., width : 2 * width]
        .astype(jnp.bfloat16)
        .reshape(row_count, length, heads, head_dim)
    )
    value_rows = (
        projected[..., 2 * width : 3 * width]
        .astype(jnp.bfloat16)
        .reshape(row_count, length, heads, head_dim)
    )
    gate_values = jax.nn.sigmoid(projected[..., 3 * width :])
    bias_rows = jnp.einsum(
        "jkc,ch->jhk", normed, weight_bias, preferred_element_type=jnp.float32
    ).astype(jnp.bfloat16)
    piece_bias = lax.all_gather(bias_rows, "dap", axis=0, tiled=True)
    piece_rows = piece_bias.shape[0]
    block_rows = math.gcd(piece_rows, 64)

    def per_one_block(block_index):
        offset = block_index * block_rows
        bias_block = lax.dynamic_slice_in_dim(piece_bias, offset, block_rows, 0).astype(jnp.float32)
        query_block = lax.dynamic_slice_in_dim(queries, offset, block_rows, 1)
        scores = (
            jnp.einsum("ijhd,ikhd->ihjk", query_block, key_rows, preferred_element_type=jnp.float32)
            * scaling
        )
        scores = (
            scores + jnp.transpose(bias_block, (1, 0, 2))[None] + mask_bias[None, None, None, :]
        )
        weights = softmax_rows(scores)
        mixed_values = jnp.einsum(
            "ihjk,ikhd->ijhd", weights, value_rows, preferred_element_type=jnp.float32
        )
        mixed_values = mixed_values.reshape(row_count, block_rows, width)
        gate_block = lax.dynamic_slice_in_dim(gate_values, offset, block_rows, 1)
        return (mixed_values * gate_block).astype(jnp.bfloat16)

    blocks = lax.map(per_one_block, jnp.arange(piece_rows // block_rows, dtype=jnp.int32))
    attended = jnp.transpose(blocks, (1, 0, 2, 3)).reshape(row_count, piece_rows, width)
    update = jnp.einsum("ijc,cd->ijd", attended, weight_final, preferred_element_type=jnp.float32)
    return (current.astype(jnp.float32) + update).astype(jnp.bfloat16)


def transition(current, trans_up, trans_down):
    normed = layer_norm(current, -1).astype(jnp.bfloat16)
    hidden = jax.nn.relu(
        jnp.einsum("ijc,cf->ijf", normed, trans_up, preferred_element_type=jnp.float32)
    ).astype(jnp.bfloat16)
    update = jnp.einsum("ijf,fc->ijc", hidden, trans_down, preferred_element_type=jnp.float32)
    return (current.astype(jnp.float32) + update).astype(jnp.bfloat16)


def ending_node(
    current, mask_bias, weight_project, weight_bias, weight_final, trans_up, trans_down
):
    columns = regroup_second(current)
    length, col_count, width = columns.shape
    heads = weight_bias.shape[1]
    head_dim = width // heads
    scaling = 1.0 / math.sqrt(head_dim)
    normed = layer_norm(columns, -1).astype(jnp.bfloat16)
    projected = jnp.einsum(
        "ijc,ce->ije", normed, weight_project, preferred_element_type=jnp.float32
    )
    queries = (
        projected[..., :width].astype(jnp.bfloat16).reshape(length, col_count, heads, head_dim)
    )
    key_cols = (
        projected[..., width : 2 * width]
        .astype(jnp.bfloat16)
        .reshape(length, col_count, heads, head_dim)
    )
    value_cols = (
        projected[..., 2 * width : 3 * width]
        .astype(jnp.bfloat16)
        .reshape(length, col_count, heads, head_dim)
    )
    gate_values = jax.nn.sigmoid(projected[..., 3 * width :])
    own_normed = layer_norm(current, -1).astype(jnp.bfloat16)
    bias_part = jnp.einsum(
        "kic,ch->khi", own_normed, weight_bias, preferred_element_type=jnp.float32
    ).astype(jnp.bfloat16)

    def bias_slice(gathered, offset, block_rows):
        return jnp.transpose(lax.dynamic_slice_in_dim(gathered, offset, block_rows, 2), (1, 2, 0))

    gathered = lax.all_gather(bias_part, "dap", axis=0, tiled=True)
    block_rows = math.gcd(length, 64)

    def ending_one_block(block_index):
        offset = block_index * block_rows
        query_block = lax.dynamic_slice_in_dim(queries, offset, block_rows, 0)
        scores = (
            jnp.einsum("ijhd,kjhd->jhik", query_block, key_cols, preferred_element_type=jnp.float32)
            * scaling
        )
        scores = (
            scores
            + bias_slice(gathered, offset, block_rows).astype(jnp.float32)[None]
            + mask_bias[None, None, None, :]
        )
        weights = softmax_rows(scores)
        mixed_values = jnp.einsum(
            "jhik,kjhd->ijhd", weights, value_cols, preferred_element_type=jnp.float32
        )
        mixed_values = mixed_values.reshape(block_rows, col_count, width)
        gate_block = lax.dynamic_slice_in_dim(gate_values, offset, block_rows, 0)
        return (mixed_values * gate_block).astype(jnp.bfloat16)

    blocks = lax.map(ending_one_block, jnp.arange(length // block_rows, dtype=jnp.int32))
    attended = blocks.reshape(length, col_count, width)
    update = jnp.einsum(
        "ijc,cd->ijd", attended, weight_final, preferred_element_type=jnp.float32
    ).astype(jnp.bfloat16)
    columns = (columns.astype(jnp.float32) + update.astype(jnp.float32)).astype(jnp.bfloat16)
    finished = return_columns(transition(columns, trans_up, trans_down))
    return finished


def local(
    pair_act,
    chain_id,
    pad_mask,
    chain_table,
    out_project,
    out_gate,
    out_final,
    in_project,
    in_gate,
    in_final,
    start_project,
    start_bias,
    start_final,
    end_project,
    end_bias,
    end_final,
    trans_up,
    trans_down,
):
    row_count = pair_act.shape[0]
    first_row = lax.axis_index("dap") * row_count
    mask_all = pad_mask.astype(jnp.float32)
    mask_rows = lax.dynamic_slice_in_dim(mask_all, first_row, row_count, 0)
    chain_rows = lax.dynamic_slice_in_dim(chain_id, first_row, row_count, 0)
    same_chain = chain_rows[:, None] == chain_id[None, :]
    chain_add = jnp.where(
        same_chain[:, :, None], chain_table[1][None, None, :], chain_table[0][None, None, :]
    )
    current = (pair_act.astype(jnp.float32) + chain_add).astype(jnp.bfloat16)
    current = triangle_product(current, mask_rows, mask_all, out_project, out_gate, out_final, True)
    current = triangle_product(current, mask_rows, mask_all, in_project, in_gate, in_final, False)
    mask_bias = (mask_all - 1.0) * mask_scale
    current = starting_node(current, mask_bias, start_project, start_bias, start_final)
    return ending_node(current, mask_bias, end_project, end_bias, end_final, trans_up, trans_down)


def solution(mesh):
    return jax.shard_map(
        local,
        mesh=mesh,
        in_specs=(
            P(("groups", "dap"), None, None),
            P("groups"),
            P("groups"),
            P(),
            P(),
            P(),
            P(),
            P(),
            P(),
            P(),
            P(),
            P(),
            P(),
            P(),
            P(),
            P(),
            P(),
            P(),
        ),
        out_specs=P(("groups", "dap"), None, None),
        check_vma=False,
    )
```

profile of v0, /device:TPU:0, one launch (start us, length us, event | category | flops | bytes accessed | tf_op | source)
XLA Modules:
  0.0 135.4 jit_solution(3977326848309386264)
XLA Ops:
  0.0 0.7 convert_element_type.196
  0.9 0.6 copy-done.15
  1.6 0.6 copy-done.5
  2.2 0.2 convert_reduce_fusion
  2.4 0.2 fusion.70
  2.6 1.1 convolution_bitcast_fusion.1
  3.8 0.1 copy.109
  3.9 0.7 reshape.256
  4.6 7.4 %all-to-all-start.1 = ((bf16[16,2,256]{2,1,0:T(2,128)(2,1)}), bf16[16,2,256]{2,1,0:T(2,128)(2,1)S(1)}, u32[]{:S(2)}, u32[]{:S(2)}) async-start(bf16[16,2,256]{2,1,0:T(2,128)(2,1)} %reshape.256), calls=%async_computation.1 | async-start | bytes 32768 | tf_op jit(solution)/shard_map/all_to_all | solution.py:54
  12.0 0.1 copy.106
  12.1 0.7 reshape.254
  12.8 5.7 %all-to-all-done.1 = bf16[16,2,256]{2,1,0:T(2,128)(2,1)S(1)} async-done(((bf16[16,2,256]{2,1,0:T(2,128)(2,1)}), bf16[16,2,256]{2,1,0:T(2,128)(2,1)S(1)}, u32[]{:S(2)}, u32[]{:S(2)}) %all-to-all-start.1) | async-done | bytes 16416 | tf_op jit(solution)/shard_map/all_to_all | solution.py:54
  18.5 3.5 %all-to-all-start = ((bf16[16,2,256]{2,1,0:T(2,128)(2,1)}), bf16[16,2,256]{2,1,0:T(2,128)(2,1)S(1)}, u32[]{:S(2)}, u32[]{:S(2)}) async-start(bf16[16,2,256]{2,1,0:T(2,128)(2,1)} %reshape.254), calls=%async_computation | async-start | bytes 32768 | tf_op jit(solution)/shard_map/all_to_all | solution.py:53
  22.2 6.3 %all-to-all-done = bf16[16,2,256]{2,1,0:T(2,128)(2,1)S(1)} async-done(((bf16[16,2,256]{2,1,0:T(2,128)(2,1)}), bf16[16,2,256]{2,1,0:T(2,128)(2,1)S(1)}, u32[]{:S(2)}, u32[]{:S(2)}) %all-to-all-start) | async-done | bytes 16416 | tf_op jit(solution)/shard_map/all_to_all | solution.py:53
  28.7 0.2 convolution_convert_fusion.1
  28.9 0.7 reshape.258
  29.6 3.6 %all-to-all-start.2 = ((bf16[16,2,256]{2,1,0:T(2,128)(2,1)}), bf16[16,2,256]{2,1,0:T(2,128)(2,1)S(1)}, u32[]{:S(2)}, u32[]{:S(2)}) async-start(bf16[16,2,256]{2,1,0:T(2,128)(2,1)} %reshape.258), calls=%async_computation.2 | async-start | bytes 32768 | tf_op jit(solution)/shard_map/all_to_all | solution.py:20
  33.2 0.2 fusion.19
  33.4 6.2 %all-to-all-done.2 = bf16[16,2,256]{2,1,0:T(2,128)(2,1)S(1)} async-done(((bf16[16,2,256]{2,1,0:T(2,128)(2,1)}), bf16[16,2,256]{2,1,0:T(2,128)(2,1)S(1)}, u32[]{:S(2)}, u32[]{:S(2)}) %all-to-all-start.2) | async-done | bytes 16416 | tf_op jit(solution)/shard_map/all_to_all | solution.py:20
  39.9 0.7 copy-done.9
  40.6 0.3 fusion.136
  40.9 0.2 multiply_reduce_fusion.2
  41.0 0.5 copy-done.2
  41.5 0.2 convolution_bitcast_fusion
  41.9 0.7 reshape.262
  42.6 3.5 %all-to-all-start.3 = ((bf16[16,2,256]{2,1,0:T(2,128)(2,1)}), bf16[16,2,256]{2,1,0:T(2,128)(2,1)S(1)}, u32[]{:S(2)}, u32[]{:S(2)}) async-start(bf16[16,2,256]{2,1,0:T(2,128)(2,1)} %reshape.262), calls=%async_computation.3 | async-start | bytes 32768 | tf_op jit(solution)/shard_map/all_to_all | solution.py:53
  46.1 0.1 copy.118
  46.3 0.7 reshape.260
  47.0 5.6 %all-to-all-done.3 = bf16[16,2,256]{2,1,0:T(2,128)(2,1)S(1)} async-done(((bf16[16,2,256]{2,1,0:T(2,128)(2,1)}), bf16[16,2,256]{2,1,0:T(2,128)(2,1)S(1)}, u32[]{:S(2)}, u32[]{:S(2)}) %all-to-all-start.3) | async-done | bytes 16416 | tf_op jit(solution)/shard_map/all_to_all | solution.py:53
  52.6 3.5 %all-to-all-start.4 = ((bf16[16,2,256]{2,1,0:T(2,128)(2,1)}), bf16[16,2,256]{2,1,0:T(2,128)(2,1)S(1)}, u32[]{:S(2)}, u32[]{:S(2)}) async-start(bf16[16,2,256]{2,1,0:T(2,128)(2,1)} %reshape.260), calls=%async_computation.4 | async-start | bytes 32768 | tf_op jit(solution)/shard_map/all_to_all | solution.py:54
  56.3 6.3 %all-to-all-done.4 = bf16[16,2,256]{2,1,0:T(2,128)(2,1)S(1)} async-done(((bf16[16,2,256]{2,1,0:T(2,128)(2,1)}), bf16[16,2,256]{2,1,0:T(2,128)(2,1)S(1)}, u32[]{:S(2)}, u32[]{:S(2)}) %all-to-all-start.4) | async-done | bytes 16416 | tf_op jit(solution)/shard_map/all_to_all | solution.py:54
  62.8 0.2 convolution_convert_fusion
  63.0 0.7 reshape.264
  63.7 3.6 %all-to-all-start.5 = ((bf16[16,2,256]{2,1,0:T(2,128)(2,1)}), bf16[16,2,256]{2,1,0:T(2,128)(2,1)S(1)}, u32[]{:S(2)}, u32[]{:S(2)}) async-start(bf16[16,2,256]{2,1,0:T(2,128)(2,1)} %reshape.264), calls=%async_computation.5 | async-start | bytes 32768 | tf_op jit(solution)/shard_map/all_to_all | solution.py:20
  67.4 0.2 fusion.15
  67.6 6.2 %all-to-all-done.5 = bf16[16,2,256]{2,1,0:T(2,128)(2,1)S(1)} async-done(((bf16[16,2,256]{2,1,0:T(2,128)(2,1)}), bf16[16,2,256]{2,1,0:T(2,128)(2,1)S(1)}, u32[]{:S(2)}, u32[]{:S(2)}) %all-to-all-start.5) | async-done | bytes 16416 | tf_op jit(solution)/shard_map/all_to_all | solution.py:20
  74.0 0.7 copy-done.4
  74.7 0.3 fusion.137
  75.0 0.2 multiply_reduce_fusion.1
  75.2 0.7 copy-done.13
  75.8 0.2 fusion.31
  76.1 17.7 %all_gather.6 = bf16[32,4,32]{2,1,0:T(4,128)(2,1)S(1)} all-gather(bf16[2,4,32]{2,1,0:T(4,128)(2,1)S(1)} %fusion.31), channel_id=1, replica_groups=mesh['groups'=2,'dap'=16] {'dap'}, dimensions={0}, use_global_device_ids=true | all-gather | bytes 8704 | tf_op jit(solution)/shard_map/all_gather | solution.py:99
  93.8 0.2 fusion.138
  94.2 0.2 fusion.7
  94.6 0.2 fusion.50
  94.8 0.7 copy-done.11
  95.5 0.2 convert_reduce_fusion.1
  95.7 0.6 copy.131
  96.4 0.2 fusion.72
  96.5 3.6 %all-to-all-start.6 = ((bf16[2,32,128]{2,0,1:T(2,128)(2,1)}), bf16[2,32,128]{2,0,1:T(2,128)(2,1)S(1)}, u32[]{:S(2)}, u32[]{:S(2)}) async-start(bf16[2,32,128]{2,0,1:T(2,128)(2,1)} %copy.131), calls=%async_computation.6 | async-start | bytes 32768 | tf_op jit(solution)/shard_map/all_to_all | solution.py:20
  100.2 0.2 fusion.32
  100.4 21.8 %all_gather.7 = bf16[32,4,32]{2,1,0:T(4,128)(2,1)S(1)} all-gather(bf16[2,4,32]{2,1,0:T(4,128)(2,1)S(1)} %fusion.32), channel_id=1, replica_groups=mesh['groups'=2,'dap'=16] {'dap'}, dimensions={0}, use_global_device_ids=true | all-gather | bytes 8704 | tf_op jit(solution)/shard_map/all_gather | solution.py:171
  122.4 0.2 fusion.104
  122.6 0.2 copy.135
  122.9 0.2 copy.138
  123.3 0.2 fusion.140
  123.7 0.2 fusion.9
  124.0 0.2 fusion.51
  124.3 0.7 copy-done.12
  125.0 0.2 fusion.142
  125.2 0.2 multiply_reduce_fusion
  125.4 0.3 fusion.30
  125.8 9.1 %all_to_all.117 = bf16[32,2,128]{2,1,0:T(2,128)(2,1)S(1)} all-to-all(bf16[32,2,128]{2,1,0:T(2,128)(2,1)S(1)} %copy.145), channel_id=1, replica_groups=mesh['groups'=2,'dap'=16] {'dap'}, dimensions={0} | all-to-all | bytes 32768 | tf_op jit(solution)/shard_map/all_to_all | solution.py:24
  134.8 0.6 copy.146
  (96 shorter events, 3.3 us)
Async XLA Ops:
  0.0 93.8 %copy-start = (bf16[128,512]{1,0:T(8,128)(2,1)S(1)}, bf16[128,512]{1,0:T(8,128)(2,1)}, u32[]{:S(2)}) copy-start(bf16[128,512]{1,0:T(8,128)(2,1)} %param.28) | copy-start | bytes 393220
  0.0 2.2 %copy-start.1 = (bf16[2,32,128]{2,1,0:T(8,128)(2,1)S(1)}, bf16[2,32,128]{2,1,0:T(8,128)(2,1)}, u32[]{:S(2)}) copy-start(bf16[2,32,128]{2,1,0:T(8,128)(2,1)} %param.18) | copy-start | bytes 49156
  0.8 0.7 copy-start.15
  1.5 0.7 copy-start.5
  4.6 13.9 %all-to-all-start.1 = ((bf16[16,2,256]{2,1,0:T(2,128)(2,1)}), bf16[16,2,256]{2,1,0:T(2,128)(2,1)S(1)}, u32[]{:S(2)}, u32[]{:S(2)}) async-start(bf16[16,2,256]{2,1,0:T(2,128)(2,1)} %reshape.256), calls=%async_computation.1 | async-start | bytes 32768 | tf_op jit(solution)/shard_map/all_to_all | solution.py:54
  18.5 10.0 %all-to-all-start = ((bf16[16,2,256]{2,1,0:T(2,128)(2,1)}), bf16[16,2,256]{2,1,0:T(2,128)(2,1)S(1)}, u32[]{:S(2)}, u32[]{:S(2)}) async-start(bf16[16,2,256]{2,1,0:T(2,128)(2,1)} %reshape.254), calls=%async_computation | async-start | bytes 32768 | tf_op jit(solution)/shard_map/all_to_all | solution.py:53
  29.6 3.6 %copy-start.8 = (bf16[128,128]{1,0:T(8,128)(2,1)S(1)}, bf16[128,128]{1,0:T(8,128)(2,1)}, u32[]{:S(2)}) copy-start(bf16[128,128]{1,0:T(8,128)(2,1)} %param.23) | copy-start | bytes 98308
  29.6 10.1 %all-to-all-start.2 = ((bf16[16,2,256]{2,1,0:T(2,128)(2,1)}), bf16[16,2,256]{2,1,0:T(2,128)(2,1)S(1)}, u32[]{:S(2)}, u32[]{:S(2)}) async-start(bf16[16,2,256]{2,1,0:T(2,128)(2,1)} %reshape.258), calls=%async_computation.2 | async-start | bytes 32768 | tf_op jit(solution)/shard_map/all_to_all | solution.py:20
  39.8 0.8 copy-start.9
  40.6 0.9 copy-start.2
  42.6 10.0 %all-to-all-start.3 = ((bf16[16,2,256]{2,1,0:T(2,128)(2,1)}), bf16[16,2,256]{2,1,0:T(2,128)(2,1)S(1)}, u32[]{:S(2)}, u32[]{:S(2)}) async-start(bf16[16,2,256]{2,1,0:T(2,128)(2,1)} %reshape.262), calls=%async_computation.3 | async-start | bytes 32768 | tf_op jit(solution)/shard_map/all_to_all | solution.py:53
  47.0 9.1 %copy-start.16 = (s32[32]{0:T(128)S(1)}, s32[32]{0:T(128)}, u32[]{:S(2)}) copy-start(s32[32]{0:T(128)} %param.20) | copy-start | bytes 388
  52.6 10.0 %all-to-all-start.4 = ((bf16[16,2,256]{2,1,0:T(2,128)(2,1)}), bf16[16,2,256]{2,1,0:T(2,128)(2,1)S(1)}, u32[]{:S(2)}, u32[]{:S(2)}) async-start(bf16[16,2,256]{2,1,0:T(2,128)(2,1)} %reshape.260), calls=%async_computation.4 | async-start | bytes 32768 | tf_op jit(solution)/shard_map/all_to_all | solution.py:54
  63.7 3.6 %copy-start.10 = (bf16[128,128]{1,0:T(8,128)(2,1)S(1)}, bf16[128,128]{1,0:T(8,128)(2,1)}, u32[]{:S(2)}) copy-start(bf16[128,128]{1,0:T(8,128)(2,1)} %param.26) | copy-start | bytes 98308
  63.7 10.1 %all-to-all-start.5 = ((bf16[16,2,256]{2,1,0:T(2,128)(2,1)}), bf16[16,2,256]{2,1,0:T(2,128)(2,1)S(1)}, u32[]{:S(2)}, u32[]{:S(2)}) async-start(bf16[16,2,256]{2,1,0:T(2,128)(2,1)} %reshape.264), calls=%async_computation.5 | async-start | bytes 32768 | tf_op jit(solution)/shard_map/all_to_all | solution.py:20
  74.0 0.8 copy-start.4
  75.2 0.7 copy-start.13
  94.8 0.8 copy-start.11
  96.5 3.7 %copy-start.14 = (bf16[128,4]{0,1:T(4,128)(2,1)S(1)}, bf16[128,4]{0,1:T(4,128)(2,1)}, u32[]{:S(2)}) copy-start(bf16[128,4]{0,1:T(4,128)(2,1)} %param.32) | copy-start | bytes 3076
  96.5 25.7 %all-to-all-start.6 = ((bf16[2,32,128]{2,0,1:T(2,128)(2,1)}), bf16[2,32,128]{2,0,1:T(2,128)(2,1)S(1)}, u32[]{:S(2)}, u32[]{:S(2)}) async-start(bf16[2,32,128]{2,0,1:T(2,128)(2,1)} %copy.131), calls=%async_computation.6 | async-start | bytes 32768 | tf_op jit(solution)/shard_map/all_to_all | solution.py:20
  122.4 0.9 copy-start.3
  124.2 0.8 copy-start.12
  124.2 1.2 copy-start.7
  124.3 1.1 copy-start.6
where the time goes:
time: 136 us; the launch traced here: 135 us
  blocking collectives  48.5 us (36%)
  waiting for transfers between devices  36.3 us (27%)
  starting transfers between devices  28.8 us (21%)
  local copies, waits for them, and re-layouts  13.8 us (10%)
  matrix products  4.89 us (4%)
  other arithmetic  2.72 us (2%)
    all_gather x1, blocking collectives, ending_node(): gathered = lax.all_gather(bias_part, 'dap', axis=0, tiled=True)  21.8 us
    all_gather x1, blocking collectives, starting_node(): piece_bias = lax.all_gather(bias_rows, 'dap', axis=0, tiled=True)  17.7 us
    all_to_all x3, waiting for transfers between devices, regroup_second(): lax.all_to_all(values, 'dap', split_axis=1, concat_axis=0, tiled=True)  12.5 us
    all_to_all x2, waiting for transfers between devices, triangle_product(): lax.all_to_all(right_side, 'dap', split_axis=0, concat_axis=1, tiled=True)  11.9 us
    all_to_all x2, waiting for transfers between devices, triangle_product(): lax.all_to_all(left_side, 'dap', split_axis=0, concat_axis=1, tiled=True)  11.9 us
    all_to_all x3, starting transfers between devices, regroup_second(): lax.all_to_all(values, 'dap', split_axis=1, concat_axis=0, tiled=True)  10.9 us
    all_to_all x2, starting transfers between devices, triangle_product(): lax.all_to_all(right_side, 'dap', split_axis=0, concat_axis=1, tiled=True)  10.9 us
    unnamed x46, local copies, waits for them, and re-layouts  10.1 us
  transfers between devices with their start and end apart: 7, of which 6 were waited for; matrix products, arithmetic and copies ran while one was open for 2% of the time, Pallas kernels for 0%

commit v1 on v0

--- a/solution.py
+++ b/solution.py
@@ -1,8 +1,11 @@
+import functools
 import math
 
 import jax
 import jax.numpy as jnp
 from jax import lax
+from jax.experimental import pallas as pl
+from jax.experimental.pallas import tpu as pltpu
 from jax.sharding import PartitionSpec as P
 
 epsilon = 1e-05
@@ -238,9 +241,421 @@
     return ending_node(current, mask_bias, end_project, end_bias, end_final, trans_up, trans_down)
 
 
+def dot(left, right):
+    return jnp.dot(left, right, preferred_element_type=jnp.float32)
+
+
+def dot_rows(left, right):
+    return lax.dot_general(
+        left, right, (((1,), (1,)), ((), ())), preferred_element_type=jnp.float32
+    )
+
+
+def halves(values):
+    high = values.astype(jnp.bfloat16)
+    low = (values - high.astype(jnp.float32)).astype(jnp.bfloat16)
+    return jnp.concatenate([high, low], axis=1)
+
+
+def sigmoid(values):
+    return 0.5 * jnp.tanh(0.5 * values) + 0.5
+
+
+def norm_rows(values, average):
+    width = values.shape[1]
+    centred = values.astype(jnp.float32) - dot(values, average[:width])
+    spread = dot(halves(centred * centred), average)
+    return (centred * lax.rsqrt(spread + epsilon)).astype(jnp.bfloat16)
+
+
+def fused_kernel(
+    devices,
+    pair_ref,
+    chain_ref,
+    mask_ref,
+    table_ref,
+    out_project_ref,
+    out_gate_ref,
+    out_final_ref,
+    in_project_ref,
+    in_gate_ref,
+    in_final_ref,
+    start_project_ref,
+    start_bias_ref,
+    start_final_ref,
+    end_project_ref,
+    end_bias_ref,
+    end_final_ref,
+    trans_up_ref,
+    trans_down_ref,
+    result_ref,
+    pair_all,
+    after_start,
+    current,
+    normed,
+    left,
+    right,
+    key_all,
+    value_all,
+    chain_wide,
+    mask_wide,
+    start_scores,
+    shift,
+    own_rows,
+    send_first,
+    recv_first,
+    send_second,
+    recv_second,
+):
+    me = lax.axis_index("dap")
+    block, width = pair_ref.shape
+    length = chain_ref.shape[1]
+    mine = block // length
+    heads = start_bias_ref.shape[1]
+    head_dim = width // heads
+    scaling = 1.0 / math.sqrt(head_dim)
+    tile = 8
+    chunks = length // tile
+    chunk_rows = tile * length
+    f32, bf16 = jnp.float32, jnp.bfloat16
+
+    barrier = pltpu.get_barrier_semaphore()
+    for step in range(1, devices):
+        peer = lax.rem(me + step, devices)
+        pl.semaphore_signal(
+            barrier, inc=1, device_id={"dap": peer}, device_id_type=pl.DeviceIdType.MESH
+        )
+    pl.semaphore_wait(barrier, devices - 1)
+
+    my_block = pl.ds(pl.multiple_of(me * block, block), block)
+
+    def exchange(source, target, send_sems, recv_sems):
+        copies = []
+        for step in range(1, devices):
+            peer = lax.rem(me + step, devices)
+            copies.append(
+                pltpu.make_async_remote_copy(
+                    src_ref=source,
+                    dst_ref=target.at[my_block],
+                    send_sem=send_sems.at[step],
+                    recv_sem=recv_sems.at[step],
+                    device_id={"dap": peer},
+                    device_id_type=pl.DeviceIdType.MESH,
+                )
+            )
+        for copy in copies:
+            copy.start()
+        return copies
+
+    copies_first = exchange(pair_ref, pair_all, send_first, recv_first)
+    pair_all[my_block, :] = pair_ref[...]
+
+    average = jnp.full((2 * width, width), 1.0 / width, bf16)
+    row_head = lax.broadcasted_iota(jnp.int32, (width, width), 0) // head_dim
+    lane_head = lax.broadcasted_iota(jnp.int32, (width, width), 1) // head_dim
+    same_head = jnp.where(row_head == lane_head, 1.0, 0.0).astype(bf16)
+    same_head_twice = jnp.concatenate([same_head, same_head], axis=0)
+    spread_heads = jnp.where(
+        lax.broadcasted_iota(jnp.int32, (heads, width), 0)
+        == lax.broadcasted_iota(jnp.int32, (heads, width), 1) // head_dim,
+        1.0,
+        0.0,
+    ).astype(bf16)
+    start_bias_wide = dot(start_bias_ref[...], spread_heads).astype(bf16)
+    end_bias_wide = dot(end_bias_ref[...], spread_heads).astype(bf16)
+    diagonal = lax.broadcasted_iota(jnp.int32, (length, length), 0) == lax.broadcasted_iota(
+        jnp.int32, (length, length), 1
+    )
+    chain_column = jnp.sum(
+        jnp.where(diagonal, chain_ref[...].astype(f32), 0.0), axis=1, keepdims=True
+    )
+    mask_column = jnp.sum(
+        jnp.where(diagonal, mask_ref[...].astype(f32), 0.0), axis=1, keepdims=True
+    )
+    chain_wide[...] = jnp.broadcast_to(chain_column, (length, width))
+    mask_all = jnp.broadcast_to(mask_column, (length, width))
+    mask_wide[...] = mask_all
+    key_lane = (
+        lax.broadcasted_iota(jnp.int32, (length, width), 1) % length
+        == lax.broadcasted_iota(jnp.int32, (length, width), 0)
+    )
+    mask_lanes = jnp.sum(jnp.where(key_lane, mask_all, 0.0), axis=0, keepdims=True)
+    key_lane_ones = jnp.where(key_lane, 1.0, 0.0)
+
+    for copy in copies_first:
+        copy.wait_recv()
+
+    def sides(chunk, normed_rows, weight_ref):
+        projected = dot(normed_rows, weight_ref[...])
+        rows_mask = mask_wide[pl.ds(chunk * tile, tile), :]
+        pair_mask = jnp.concatenate(
+            [mask_all * rows_mask[row : row + 1, :] for row in range(tile)], axis=0
+        )
+        left_side = pair_mask * sigmoid(projected[:, width : 2 * width]) * projected[:, :width]
+        right_side = (
+            pair_mask
+            * sigmoid(projected[:, 3 * width :])
+            * projected[:, 2 * width : 3 * width]
+        )
+        return left_side.astype(bf16).astype(f32), right_side.astype(bf16).astype(f32)
+
+    def first(chunk, carry):
+        rows = pl.ds(pl.multiple_of(chunk * chunk_rows, chunk_rows), chunk_rows)
+        chain_rows = chain_wide[pl.ds(chunk * tile, tile), :]
+        chain_all = chain_wide[...]
+        within = table_ref[1:2, :]
+        across = table_ref[0:1, :]
+        added = jnp.concatenate(
+            [
+                jnp.where(chain_all == chain_rows[row : row + 1, :], within, across)
+                for row in range(tile)
+            ],
+            axis=0,
+        )
+        start = (pair_all[rows, :].astype(f32) + added).astype(bf16)
+        current[rows, :] = start
+        rows_normed = norm_rows(start, average)
+        normed[rows, :] = rows_normed
+        left_side, right_side = sides(chunk, rows_normed, out_project_ref)
+        left[rows, :] = left_side
+        right[rows, :] = right_side
+        return carry
+
+    lax.fori_loop(0, chunks, first, 0)
+
+    def finish(rows, combined, gate_ref, final_ref):
+        combined_normed = norm_rows(combined.astype(bf16), average)
+        update = dot(combined_normed, final_ref[...])
+        gate = sigmoid(dot(normed[rows, :], gate_ref[...]))
+        return (current[rows, :].astype(f32) + gate * update).astype(bf16)
+
+    def outgoing(chunk, carry):
+        rows = pl.ds(pl.multiple_of(chunk * chunk_rows, chunk_rows), chunk_rows)
+
+        def add(step, totals):
+            totals = list(totals)
+            tiles = [
+                left[pl.ds(pl.multiple_of((chunk * tile + row) * length + step * tile, tile), tile), :]
+                for row in range(tile)
+            ]
+            for offset in range(tile):
+                others = right[pl.ds(step * tile + offset, length, stride=length), :]
+                for row in range(tile):
+                    totals[row] = totals[row] + tiles[row][offset : offset + 1, :] * others
+            return tuple(totals)
+
+        totals = lax.fori_loop(
+            0, chunks, add, tuple(jnp.zeros((length, width), f32) for _ in range(tile))
+        )
+        combined = jnp.concatenate(totals, axis=0)
+        updated = finish(rows, combined, out_gate_ref, out_final_ref)
+        current[rows, :] = updated
+        return carry
+
+    lax.fori_loop(0, chunks, outgoing, 0)
+
+    def second(chunk, carry):
+        rows = pl.ds(pl.multiple_of(chunk * chunk_rows, chunk_rows), chunk_rows)
+        rows_normed = norm_rows(current[rows, :], average)
+        normed[rows, :] = rows_normed
+        left_side, right_side = sides(chunk, rows_normed, in_project_ref)
+        left[rows, :] = left_side
+        right[rows, :] = right_side
+        return carry
+
+    lax.fori_loop(0, chunks, second, 0)
+
+    def incoming(chunk, carry):
+        rows = pl.ds(pl.multiple_of(chunk * chunk_rows, chunk_rows), chunk_rows)
+
+        def add(step, totals):
+            totals = list(totals)
+            for offset in range(tile):
+                base = (step * tile + offset) * length
+                own = left[pl.ds(pl.multiple_of(base + chunk * tile, tile), tile), :]
+                others = right[pl.ds(pl.multiple_of(base, length), length), :]
+                for row in range(tile):
+                    totals[row] = totals[row] + own[row : row + 1, :] * others
+            return tuple(totals)
+
+        totals = lax.fori_loop(
+            0, chunks, add, tuple(jnp.zeros((length, width), f32) for _ in range(tile))
+        )
+        combined = jnp.concatenate(totals, axis=0)
+        updated = finish(rows, combined, in_gate_ref, in_final_ref)
+        current[rows, :] = updated
+        rows_normed = norm_rows(updated, average)
+        bias = dot(rows_normed, start_bias_wide)
+        bias = jnp.concatenate(
+            [
+                jnp.sum(
+                    bias[row * length : (row + 1) * length, :] * key_lane_ones,
+                    axis=0,
+                    keepdims=True,
+                )
+                for row in range(tile)
+            ],
+            axis=0,
+        )
+        start_scores[pl.ds(pl.multiple_of(chunk * tile, tile), tile), :] = bias.astype(
+            bf16
+        ).astype(f32)
+        return carry
+
+    lax.fori_loop(0, chunks, incoming, 0)
+
+    before = current[my_block, :]
+    projected = dot(norm_rows(before, average), start_project_ref[...])
+    gates = sigmoid(projected[:, 3 * width :])
+    shared = start_scores[...] + (mask_lanes - 1.0) * mask_scale
+    lane_of_head = lax.broadcasted_iota(jnp.int32, (length, width), 1) // length
+    attended = []
+    for row in range(mine):
+        rows = slice(row * length, (row + 1) * length)
+        queries = projected[rows, :width].astype(bf16)
+        keys = projected[rows, width : 2 * width].astype(bf16)
+        values = projected[rows, 2 * width : 3 * width].astype(bf16)
+        keys = jnp.concatenate([keys] * heads, axis=0) * same_head
+        values = jnp.concatenate([values] * heads, axis=0) * same_head
+        scores = dot_rows(queries, keys) * scaling + shared
+        top = jnp.zeros_like(scores)
+        for head in range(heads):
+            own_lanes = lane_of_head == head
+            peak = jnp.max(jnp.where(own_lanes, scores, -jnp.inf), axis=1, keepdims=True)
+            top = jnp.where(own_lanes, peak, top)
+        weights = jnp.exp(scores - top)
+        total = dot(halves(weights), same_head_twice)
+        weights = (weights / total).astype(bf16)
+        attended.append((dot(weights, values) * gates[rows, :]).astype(bf16))
+    update = dot(jnp.concatenate(attended, axis=0), start_final_ref[...])
+    own_rows[...] = (before.astype(f32) + update).astype(bf16)
+
+    copies_second = exchange(own_rows, after_start, send_second, recv_second)
+    own = own_rows[...]
+    after_start[my_block, :] = own
+    own_projected = dot(norm_rows(own, average), end_project_ref[...])
+    for copy in copies_second:
+        copy.wait_recv()
+
+    def columns(chunk, carry):
+        rows = pl.ds(pl.multiple_of(chunk * chunk_rows, chunk_rows), chunk_rows)
+        rows_normed = norm_rows(after_start[rows, :], average)
+        projected = dot(rows_normed, end_project_ref[:, width : 3 * width])
+        key_all[rows, :] = projected[:, :width].astype(bf16).astype(f32)
+        value_all[rows, :] = projected[:, width:].astype(bf16).astype(f32)
+        left[rows, :] = dot(rows_normed, end_bias_wide).astype(bf16).astype(f32)
+        return carry
+
+    lax.fori_loop(0, chunks, columns, 0)
+    gates = sigmoid(own_projected[:, 3 * width :])
+    attended = []
+    for row in range(mine):
+        rows = slice(row * length, (row + 1) * length)
+        queries = own_projected[rows, :width].astype(bf16).astype(f32)
+        shared = left[pl.ds(me * mine + row, length, stride=length), :] + (
+            mask_all - 1.0
+        ) * mask_scale
+        shift[...] = shared
+        queries = jnp.concatenate([queries] * tile, axis=0)
+
+        def score(step, top):
+            rows = pl.ds(pl.multiple_of(step * chunk_rows, chunk_rows), chunk_rows)
+            products = queries * key_all[rows, :]
+            scores = dot(halves(products), same_head_twice) * scaling
+            shifts = shift[pl.ds(pl.multiple_of(step * tile, tile), tile), :]
+            for part in range(tile):
+                piece = scores[part * length : (part + 1) * length, :] + shifts[part : part + 1, :]
+                top = jnp.maximum(top, piece)
+                right[
+                    pl.ds(pl.multiple_of(step * chunk_rows + part * length, length), length), :
+                ] = piece
+            return top
+
+        top = lax.fori_loop(0, chunks, score, jnp.full((length, width), -jnp.inf, f32))
+
+        def mix(step, totals):
+            total, mixed = totals
+            for part in range(tile):
+                rows = pl.ds(pl.multiple_of(step * chunk_rows + part * length, length), length)
+                weights = jnp.exp(right[rows, :] - top)
+                total = total + weights
+                mixed = mixed + weights * value_all[rows, :]
+            return total, mixed
+
+        zero = jnp.zeros((length, width), f32)
+        total, mixed = lax.fori_loop(0, chunks, mix, (zero, zero))
+        attended.append((mixed / total * gates[slice(row * length, (row + 1) * length), :]).astype(bf16))
+    update = dot(jnp.concatenate(attended, axis=0), end_final_ref[...]).astype(bf16)
+    after_end = (own.astype(f32) + update.astype(f32)).astype(bf16)
+
+    hidden = dot(norm_rows(after_end, average), trans_up_ref[...])
+    hidden = jnp.maximum(hidden, 0.0).astype(bf16)
+    update = dot(hidden, trans_down_ref[...])
+    result_ref[...] = (after_end.astype(f32) + update).astype(bf16)
+
+    for copy in copies_first + copies_second:
+        copy.wait_send()
+
+
+def fused(devices, pair_act, chain_id, pad_mask, *weights):
+    mine, length, width = pair_act.shape
+    block = mine * length
+    pairs = length * length
+    bf16, f32 = jnp.bfloat16, jnp.float32
+    result = pl.pallas_call(
+        functools.partial(fused_kernel, devices),
+        out_shape=jax.ShapeDtypeStruct((block, width), bf16),
+        in_specs=[pl.BlockSpec(memory_space=pltpu.VMEM)] * (3 + len(weights)),
+        out_specs=pl.BlockSpec(memory_space=pltpu.VMEM),
+        scratch_shapes=[
+            pltpu.VMEM((pairs, width), bf16),
+            pltpu.VMEM((pairs, width), bf16),
+            pltpu.VMEM((pairs, width), bf16),
+            pltpu.VMEM((pairs, width), bf16),
+            pltpu.VMEM((pairs, width), f32),
+            pltpu.VMEM((pairs, width), f32),
+            pltpu.VMEM((pairs, width), f32),
+            pltpu.VMEM((pairs, width), f32),
+            pltpu.VMEM((length, width), f32),
+            pltpu.VMEM((length, width), f32),
+            pltpu.VMEM((length, width), f32),
+            pltpu.VMEM((length, width), f32),
+            pltpu.VMEM((block, width), bf16),
+            pltpu.SemaphoreType.DMA((devices,)),
+            pltpu.SemaphoreType.DMA((devices,)),
+            pltpu.SemaphoreType.DMA((devices,)),
+            pltpu.SemaphoreType.DMA((devices,)),
+        ],
+        compiler_params=pltpu.CompilerParams(
+            collective_id=0, has_side_effects=True, vmem_limit_bytes=24 * 1024 * 1024
+        ),
+    )(
+        pair_act.reshape(block, width),
+        chain_id.reshape(1, length),
+        pad_mask.reshape(1, length),
+        *weights,
+    )
+    return result.reshape(mine, length, width)
+
+
 def solution(mesh):
+    devices = mesh.shape["dap"]
+
+    def per_device(pair_act, chain_id, pad_mask, chain_table, *weights):
+        mine, length, width = pair_act.shape
+        heads = weights[7].shape[1]
+        fits = (
+            heads * length == width
+            and width // heads == length
+            and mine * devices == length
+            and (mine * length) % 16 == 0
+        )
+        if fits:
+            return fused(devices, pair_act, chain_id, pad_mask, chain_table, *weights)
+        return local(pair_act, chain_id, pad_mask, chain_table, *weights)
+
     return jax.shard_map(
-        local,
+        per_device,
         mesh=mesh,
         in_specs=(
             P(("groups", "dap"), None, None),

time: 136 us -> 49.3 us (0.36)
  blocking collectives: 48.5 us -> 0 us
  Pallas kernels: 0 us -> 37.3 us
  waiting for transfers between devices: 36.3 us -> 0 us
  starting transfers between devices: 28.8 us -> 0 us
  matrix products: 4.89 us -> 0 us
  other arithmetic: 2.72 us -> 0 us
  local copies, waits for them, and re-layouts: 13.8 us -> 11.3 us
    all_gather x2 -> x0, blocking collectives: 39.4 us -> none  [the longest x1 21.8 us: ending_node(): gathered = lax.all_gather(bias_part, 'dap', axis=0, tiled=True)]
    pallas_call x0 -> x1, Pallas kernels: none -> 37.3 us  [fused(): pl.pallas_call(functools.partial(fused_kernel, devices), out_shape=jax.Sh...]
    all_to_all x7 -> x0, waiting for transfers between devices: 36.3 us -> none  [the longest x3 12.5 us: regroup_second(): lax.all_to_all(values, 'dap', split_axis=1, concat_axis=0, tiled=True)]
    all_to_all x7 -> x0, starting transfers between devices: 28.8 us -> none  [the longest x3 10.9 us: regroup_second(): lax.all_to_all(values, 'dap', split_axis=1, concat_axis=0, tiled=True)]
    all_to_all x1 -> x0, blocking collectives: 9.07 us -> none  [return_columns(): lax.all_to_all(values, 'dap', split_axis=0, concat_axis=1, tiled=True)]
    dot_general x19 -> x0, matrix products: 4.89 us -> none  [the longest x2 1.32 us: triangle_product(): jnp.einsum('ilc,ce->eil', normed, weight_project, preferred_element_type=...]
    reduce_sum x12 -> x0, other arithmetic: 1.39 us -> none  [the longest x8 1.06 us: layer_norm(): spread = jnp.mean(centred * centred, axis=along_axis, keepdims=True)]
    unnamed x46 -> x39, local copies, waits for them, and re-layouts: 10.1 us -> 11.3 us
  transfers between devices with their start and end apart: 7 -> 0, of which waited for: 6 -> 0; matrix products, arithmetic and copies ran while one was open for 2% -> 0% of each run, Pallas kernels for 0% -> 0%
where the time goes in v1:
time: 49.3 us; the launch traced here: 48.6 us
  Pallas kernels  37.3 us (76%)
  local copies, waits for them, and re-layouts  11.3 us (23%)
    pallas_call x1, Pallas kernels, fused(): pl.pallas_call(functools.partial(fused_kernel, devices), out_shape=jax.Sh...  37.3 us
    unnamed x39, local copies, waits for them, and re-layouts  11.3 us

profile of v1, /device:TPU:0, one launch (start us, length us, event | category | flops | bytes accessed | tf_op | source)
XLA Modules:
  0.0 48.6 jit_solution(123107177877301645)
XLA Ops:
  0.0 0.0 copy-start.17
  0.0 0.0 copy-start.16
  0.0 0.7 %copy-done.16 = bf16[128,4]{0,1:T(4,128)(2,1)S(1)} copy-done((bf16[128,4]{0,1:T(4,128)(2,1)S(1)}, bf16[128,4]{0,1:T(4,128)(2,1)}, u32[]{:S(2)}) %copy-start.16) | copy-done | bytes 1048
  0.7 0.0 copy-start.6
  0.7 0.0 copy-start.7
  0.7 0.1 copy.19.start_bias_ref
  0.8 0.0 copy-done.17
  0.8 0.0 copy-start.13
  0.8 0.0 copy-start.14
  0.9 0.0 copy-start.15
  0.9 0.1 copy.20.end_bias_ref
  1.0 0.4 copy-done.6
  1.5 0.0 copy-done.7
  1.5 0.1 copy-done.13
  1.5 0.0 copy-done.14
  1.5 0.0 copy-done.15
  1.5 0.0 copy-start
  1.5 0.9 %copy-done = bf16[128,512]{1,0:T(8,128)(2,1)S(1)} copy-done((bf16[128,512]{1,0:T(8,128)(2,1)S(1)}, bf16[128,512]{1,0:T(8,128)(2,1)}, u32[]{:S(2)}) %copy-start) | copy-done | bytes 131096
  2.4 0.0 copy-start.1
  2.4 0.9 %copy-done.1 = bf16[128,512]{1,0:T(8,128)(2,1)S(1)} copy-done((bf16[128,512]{1,0:T(8,128)(2,1)S(1)}, bf16[128,512]{1,0:T(8,128)(2,1)}, u32[]{:S(2)}) %copy-start.1) | copy-done | bytes 131096
  3.3 0.0 copy-start.2
  3.3 0.9 %copy-done.2 = bf16[128,512]{1,0:T(8,128)(2,1)S(1)} copy-done((bf16[128,512]{1,0:T(8,128)(2,1)S(1)}, bf16[128,512]{1,0:T(8,128)(2,1)}, u32[]{:S(2)}) %copy-start.2) | copy-done | bytes 131096
  4.2 0.0 copy-start.3
  4.3 0.9 %copy-done.3 = bf16[128,512]{1,0:T(8,128)(2,1)S(1)} copy-done((bf16[128,512]{1,0:T(8,128)(2,1)S(1)}, bf16[128,512]{1,0:T(8,128)(2,1)}, u32[]{:S(2)}) %copy-start.3) | copy-done | bytes 131096
  5.2 0.0 copy-start.4
  5.2 0.9 %copy-done.4 = bf16[128,512]{1,0:T(8,128)(2,1)S(1)} copy-done((bf16[128,512]{1,0:T(8,128)(2,1)S(1)}, bf16[128,512]{1,0:T(8,128)(2,1)}, u32[]{:S(2)}) %copy-start.4) | copy-done | bytes 131096
  6.1 0.0 copy-start.5
  6.1 0.9 %copy-done.5 = bf16[512,128]{1,0:T(8,128)(2,1)S(1)} copy-done((bf16[512,128]{1,0:T(8,128)(2,1)S(1)}, bf16[512,128]{1,0:T(8,128)(2,1)}, u32[]{:S(2)}) %copy-start.5) | copy-done | bytes 131096
  7.0 0.0 copy-start.8
  7.0 0.8 %copy-done.8 = bf16[128,128]{1,0:T(8,128)(2,1)S(1)} copy-done((bf16[128,128]{1,0:T(8,128)(2,1)S(1)}, bf16[128,128]{1,0:T(8,128)(2,1)}, u32[]{:S(2)}) %copy-start.8) | copy-done | bytes 32792
  7.7 0.0 copy-start.9
  7.7 0.8 %copy-done.9 = bf16[128,128]{1,0:T(8,128)(2,1)S(1)} copy-done((bf16[128,128]{1,0:T(8,128)(2,1)S(1)}, bf16[128,128]{1,0:T(8,128)(2,1)}, u32[]{:S(2)}) %copy-start.9) | copy-done | bytes 32792
  8.5 0.0 copy-start.10
  8.5 0.8 %copy-done.10 = bf16[128,128]{1,0:T(8,128)(2,1)S(1)} copy-done((bf16[128,128]{1,0:T(8,128)(2,1)S(1)}, bf16[128,128]{1,0:T(8,128)(2,1)}, u32[]{:S(2)}) %copy-start.10) | copy-done | bytes 32792
  9.2 0.0 copy-start.11
  9.2 0.8 %copy-done.11 = bf16[128,128]{1,0:T(8,128)(2,1)S(1)} copy-done((bf16[128,128]{1,0:T(8,128)(2,1)S(1)}, bf16[128,128]{1,0:T(8,128)(2,1)}, u32[]{:S(2)}) %copy-start.11) | copy-done | bytes 32792
  10.0 0.0 copy-start.12
  10.0 0.7 %copy-done.12 = bf16[2,32,128]{2,1,0:T(8,128)(2,1)S(1)} copy-done((bf16[2,32,128]{2,1,0:T(8,128)(2,1)S(1)}, bf16[2,32,128]{2,1,0:T(8,128)(2,1)}, u32[]{:S(2)}) %copy-start.12) | copy-done | bytes 16408
  10.7 37.3 %shard_map.172 = bf16[64,128]{1,0:T(8,128)(2,1)S(1)} custom-call(bf16[64,128]{1,0:T(8,128)(2,1)S(1)} %bitcast.5, s32[1,32]{1,0:T(1,128)S(1)} %bitcast.6, s32[1,32]{1,0:T(1,128)S(1)} %bitcast.7, f32[2,128]{1,0:T(2,128)S(1)} %copy-done.13, bf16[128,512]{1,0:T(8,128)(2,1)S(1)} %copy-done, bf16[128,128]{1,0:T(8,128)(2,1)S(1)} %copy-done.6, ...), custom_call_target="tpu_custom_call" | custom-call | tf_op jit(solution)/shard_map/pallas_call | solution.py:605
  48.0 0.6 %copy.22 = bf16[2,32,128]{2,1,0:T(8,128)(2,1)} copy(bf16[2,32,128]{2,1,0:T(8,128)(2,1)S(1)} %bitcast.4) | data formatting | bytes 32768
Async XLA Ops:
  0.0 0.8 %copy-start.17 = (bf16[128,4]{0,1:T(4,128)(2,1)S(1)}, bf16[128,4]{0,1:T(4,128)(2,1)}, u32[]{:S(2)}) copy-start(bf16[128,4]{0,1:T(4,128)(2,1)} %param.32) | copy-start | bytes 3076
  0.0 0.7 %copy-start.16 = (bf16[128,4]{0,1:T(4,128)(2,1)S(1)}, bf16[128,4]{0,1:T(4,128)(2,1)}, u32[]{:S(2)}) copy-start(bf16[128,4]{0,1:T(4,128)(2,1)} %param.29) | copy-start | bytes 3076
  0.7 0.8 %copy-start.6 = (bf16[128,128]{1,0:T(8,128)(2,1)S(1)}, bf16[128,128]{1,0:T(8,128)(2,1)}, u32[]{:S(2)}) copy-start(bf16[128,128]{1,0:T(8,128)(2,1)} %out_gate_ref.1) | copy-start | bytes 98308
  0.7 0.8 %copy-start.7 = (bf16[128,128]{1,0:T(8,128)(2,1)S(1)}, bf16[128,128]{1,0:T(8,128)(2,1)}, u32[]{:S(2)}) copy-start(bf16[128,128]{1,0:T(8,128)(2,1)} %out_final_ref.1) | copy-start | bytes 98308
  0.8 0.7 %copy-start.13 = (f32[2,128]{1,0:T(2,128)S(1)}, f32[2,128]{1,0:T(2,128)}, u32[]{:S(2)}) copy-start(f32[2,128]{1,0:T(2,128)} %table_ref.1) | copy-start | bytes 3076
  0.8 0.7 %copy-start.14 = (s32[32]{0:T(128)S(1)}, s32[32]{0:T(128)}, u32[]{:S(2)}) copy-start(s32[32]{0:T(128)} %param.19) | copy-start | bytes 388
  0.9 0.7 %copy-start.15 = (s32[32]{0:T(128)S(1)}, s32[32]{0:T(128)}, u32[]{:S(2)}) copy-start(s32[32]{0:T(128)} %param.20) | copy-start | bytes 388
  1.5 0.9 %copy-start = (bf16[128,512]{1,0:T(8,128)(2,1)S(1)}, bf16[128,512]{1,0:T(8,128)(2,1)}, u32[]{:S(2)}) copy-start(bf16[128,512]{1,0:T(8,128)(2,1)} %out_project_ref.1) | copy-start | bytes 393220
  2.4 0.9 %copy-start.1 = (bf16[128,512]{1,0:T(8,128)(2,1)S(1)}, bf16[128,512]{1,0:T(8,128)(2,1)}, u32[]{:S(2)}) copy-start(bf16[128,512]{1,0:T(8,128)(2,1)} %in_project_ref.1) | copy-start | bytes 393220
  3.3 0.9 %copy-start.2 = (bf16[128,512]{1,0:T(8,128)(2,1)S(1)}, bf16[128,512]{1,0:T(8,128)(2,1)}, u32[]{:S(2)}) copy-start(bf16[128,512]{1,0:T(8,128)(2,1)} %start_project_ref.1) | copy-start | bytes 393220
  4.2 0.9 %copy-start.3 = (bf16[128,512]{1,0:T(8,128)(2,1)S(1)}, bf16[128,512]{1,0:T(8,128)(2,1)}, u32[]{:S(2)}) copy-start(bf16[128,512]{1,0:T(8,128)(2,1)} %end_project_ref.1) | copy-start | bytes 393220
  5.2 0.9 %copy-start.4 = (bf16[128,512]{1,0:T(8,128)(2,1)S(1)}, bf16[128,512]{1,0:T(8,128)(2,1)}, u32[]{:S(2)}) copy-start(bf16[128,512]{1,0:T(8,128)(2,1)} %trans_up_ref.1) | copy-start | bytes 393220
  6.1 0.9 %copy-start.5 = (bf16[512,128]{1,0:T(8,128)(2,1)S(1)}, bf16[512,128]{1,0:T(8,128)(2,1)}, u32[]{:S(2)}) copy-start(bf16[512,128]{1,0:T(8,128)(2,1)} %trans_down_ref.1) | copy-start | bytes 393220
  7.0 0.8 %copy-start.8 = (bf16[128,128]{1,0:T(8,128)(2,1)S(1)}, bf16[128,128]{1,0:T(8,128)(2,1)}, u32[]{:S(2)}) copy-start(bf16[128,128]{1,0:T(8,128)(2,1)} %in_gate_ref.1) | copy-start | bytes 98308
  7.7 0.8 %copy-start.9 = (bf16[128,128]{1,0:T(8,128)(2,1)S(1)}, bf16[128,128]{1,0:T(8,128)(2,1)}, u32[]{:S(2)}) copy-start(bf16[128,128]{1,0:T(8,128)(2,1)} %in_final_ref.1) | copy-start | bytes 98308
  8.5 0.8 %copy-start.10 = (bf16[128,128]{1,0:T(8,128)(2,1)S(1)}, bf16[128,128]{1,0:T(8,128)(2,1)}, u32[]{:S(2)}) copy-start(bf16[128,128]{1,0:T(8,128)(2,1)} %start_final_ref.1) | copy-start | bytes 98308
  9.2 0.8 %copy-start.11 = (bf16[128,128]{1,0:T(8,128)(2,1)S(1)}, bf16[128,128]{1,0:T(8,128)(2,1)}, u32[]{:S(2)}) copy-start(bf16[128,128]{1,0:T(8,128)(2,1)} %end_final_ref.1) | copy-start | bytes 98308
  10.0 0.7 %copy-start.12 = (bf16[2,32,128]{2,1,0:T(8,128)(2,1)S(1)}, bf16[2,32,128]{2,1,0:T(8,128)(2,1)}, u32[]{:S(2)}) copy-start(bf16[2,32,128]{2,1,0:T(8,128)(2,1)} %param.18) | copy-start | bytes 49156

commit v2 on v1

--- a/solution.py
+++ b/solution.py
@@ -251,6 +251,12 @@
     )
 
 
+def dot_columns(left, right):
+    return lax.dot_general(
+        left, right, (((0,), (0,)), ((), ())), preferred_element_type=jnp.float32
+    )
+
+
 def halves(values):
     high = values.astype(jnp.bfloat16)
     low = (values - high.astype(jnp.float32)).astype(jnp.bfloat16)
@@ -270,48 +276,61 @@
 
 def fused_kernel(
     devices,
-    pair_ref,
-    chain_ref,
-    mask_ref,
-    table_ref,
-    out_project_ref,
-    out_gate_ref,
-    out_final_ref,
-    in_project_ref,
-    in_gate_ref,
-    in_final_ref,
-    start_project_ref,
-    start_bias_ref,
-    start_final_ref,
-    end_project_ref,
-    end_bias_ref,
-    end_final_ref,
-    trans_up_ref,
-    trans_down_ref,
-    result_ref,
-    pair_all,
-    after_start,
-    current,
-    normed,
-    left,
-    right,
-    key_all,
-    value_all,
-    chain_wide,
-    mask_wide,
-    start_scores,
-    shift,
-    own_rows,
-    send_first,
-    recv_first,
-    send_second,
-    recv_second,
+    count,
+    *refs,
 ):
+    sources, result_ref, held = refs[:count], refs[count], refs[count + 1 : 2 * count + 1]
+    (
+        pair_ref,
+        chain_ref,
+        mask_ref,
+        table_ref,
+        out_project_ref,
+        out_gate_ref,
+        out_final_ref,
+        in_project_ref,
+        in_gate_ref,
+        in_final_ref,
+        start_project_ref,
+        start_bias_ref,
+        start_final_ref,
+        end_project_ref,
+        end_bias_ref,
+        end_final_ref,
+        trans_up_ref,
+        trans_down_ref,
+    ) = held
+    (
+        pair_all,
+        after_start,
+        current,
+        normed,
+        left,
+        right,
+        key_all,
+        value_all,
+        chain_wide,
+        mask_wide,
+        start_scores,
+        shift,
+        own_rows,
+        send_first,
+        recv_first,
+        send_second,
+        recv_second,
+        load_sem,
+    ) = refs[2 * count + 1 :]
+    loads = [
+        pltpu.make_async_copy(source, target, load_sem.at[index])
+        for index, (source, target) in enumerate(zip(sources, held))
+    ]
+    for load in loads:
+        load.start()
     me = lax.axis_index("dap")
     block, width = pair_ref.shape
     length = chain_ref.shape[1]
     mine = block // length
-    heads = start_bias_ref.shape[1]
+    heads = start_bias_ref.shape[0]
     head_dim = width // heads
     scaling = 1.0 / math.sqrt(head_dim)
     tile = 8
@@ -347,8 +366,12 @@
             copy.start()
         return copies
 
+    loads[0].wait()
     copies_first = exchange(pair_ref, pair_all, send_first, recv_first)
     pair_all[my_block, :] = pair_ref[...]
+
+    for load in loads[1:]:
+        load.wait()
 
     average = jnp.full((2 * width, width), 1.0 / width, bf16)
     row_head = lax.broadcasted_iota(jnp.int32, (width, width), 0) // head_dim
@@ -361,8 +384,8 @@
         1.0,
         0.0,
     ).astype(bf16)
-    start_bias_wide = dot(start_bias_ref[...], spread_heads).astype(bf16)
-    end_bias_wide = dot(end_bias_ref[...], spread_heads).astype(bf16)
+    start_bias_wide = dot_columns(start_bias_ref[...], spread_heads).astype(bf16)
+    end_bias_wide = dot_columns(end_bias_ref[...], spread_heads).astype(bf16)
     diagonal = lax.broadcasted_iota(jnp.int32, (length, length), 0) == lax.broadcasted_iota(
         jnp.int32, (length, length), 1
     )
@@ -602,12 +625,25 @@
     block = mine * length
     pairs = length * length
     bf16, f32 = jnp.bfloat16, jnp.float32
+    start_bias, end_bias = weights[8], weights[11]
+    operands = (
+        pair_act.reshape(block, width),
+        chain_id.reshape(1, length),
+        pad_mask.reshape(1, length),
+        *weights[:8],
+        start_bias.T,
+        *weights[9:11],
+        end_bias.T,
+        *weights[12:],
+    )
+    count = len(operands)
     result = pl.pallas_call(
-        functools.partial(fused_kernel, devices),
+        functools.partial(fused_kernel, devices, count),
         out_shape=jax.ShapeDtypeStruct((block, width), bf16),
-        in_specs=[pl.BlockSpec(memory_space=pltpu.VMEM)] * (3 + len(weights)),
+        in_specs=[pl.BlockSpec(memory_space=pltpu.HBM)] * count,
         out_specs=pl.BlockSpec(memory_space=pltpu.VMEM),
-        scratch_shapes=[
+        scratch_shapes=[pltpu.VMEM(operand.shape, operand.dtype) for operand in operands]
+        + [
             pltpu.VMEM((pairs, width), bf16),
             pltpu.VMEM((pairs, width), bf16),
             pltpu.VMEM((pairs, width), bf16),
@@ -625,16 +661,12 @@
             pltpu.SemaphoreType.DMA((devices,)),
             pltpu.SemaphoreType.DMA((devices,)),
             pltpu.SemaphoreType.DMA((devices,)),
+            pltpu.SemaphoreType.DMA((count,)),
         ],
         compiler_params=pltpu.CompilerParams(
-            collective_id=0, has_side_effects=True, vmem_limit_bytes=24 * 1024 * 1024
+            collective_id=0, has_side_effects=True, vmem_limit_bytes=60 * 1024 * 1024
         ),
-    )(
-        pair_act.reshape(block, width),
-        chain_id.reshape(1, length),
-        pad_mask.reshape(1, length),
-        *weights,
-    )
+    )(*operands)
     return result.reshape(mine, length, width)
 
 

time: 49.3 us -> 39.7 us (0.81)
  local copies, waits for them, and re-layouts: 11.3 us -> 1.32 us
  Pallas kernels: 37.3 us -> 38.1 us
    unnamed x39 -> x1, local copies, waits for them, and re-layouts: 11.3 us -> 1.32 us
    pallas_call x1, Pallas kernels: 37.3 us -> 38.1 us  [fused(): pl.pallas_call(functools.partial(fused_kernel, devices, count), out_shape...]
where the time goes in v2:
time: 39.7 us; the launch traced here: 39.5 us
  Pallas kernels  38.1 us (96%)
  local copies, waits for them, and re-layouts  1.32 us (3%)
    pallas_call x1, Pallas kernels, fused(): pl.pallas_call(functools.partial(fused_kernel, devices, count), out_shape...  38.1 us
    unnamed x1, local copies, waits for them, and re-layouts  1.32 us

profile of v2, /device:TPU:0, one launch (start us, length us, event | category | flops | bytes accessed | tf_op | source)
XLA Modules:
  0.0 39.5 jit_solution(10802829299295550853)
XLA Ops:
  0.0 38.1 %shard_map.172 = bf16[64,128]{1,0:T(8,128)(2,1)} custom-call(bf16[64,128]{1,0:T(8,128)(2,1)} %bitcast.7, s32[1,32]{1,0:T(1,128)} %bitcast.10, s32[1,32]{1,0:T(1,128)} %bitcast.11, f32[2,128]{1,0:T(2,128)} %refs_3_.1, bf16[128,512]{1,0:T(8,128)(2,1)} %refs_4_.1, bf16[128,128]{1,0:T(8,128)(2,1)} %refs_5_.1, bf16[128,128]{1,0:T(8,128)(2,1)} %refs_6_.1, ...), custom_call_target="tpu_custom_call" | custom-call | tf_op jit(solution)/shard_map/pallas_call | solution.py:640
  38.1 1.3 %copy.20 = bf16[2,32,128]{2,1,0:T(8,128)(2,1)} copy(bf16[2,32,128]{2,1,0:T(8,128)(2,1)} %bitcast.6) | data formatting | bytes 32768

commit v3 on v2

--- a/solution.py
+++ b/solution.py
@@ -367,6 +367,27 @@
         return copies
 
     loads[0].wait()
+    def arrivals(target, send_sems, recv_sems, order):
+        together = chunk_rows // block
+        place, chunk, bit = me // together, 0, 1
+        while bit < chunks:
+            has = lax.rem(place // bit, 2)
+            chunk = chunk + (1 - has if (order // bit) % 2 else has) * bit
+            bit *= 2
+        for member in range(1 if order == 0 else 0, together):
+            source = chunk * together + lax.rem(me + member, together)
+            step = lax.rem(me - source + devices, devices)
+            landed = pl.ds(pl.multiple_of(source * block, block), block)
+            pltpu.make_async_remote_copy(
+                src_ref=target.at[landed],
+                dst_ref=target.at[landed],
+                send_sem=send_sems.at[step],
+                recv_sem=recv_sems.at[step],
+                device_id={"dap": source},
+                device_id_type=pl.DeviceIdType.MESH,
+            ).wait_recv()
+        return chunk
+
     copies_first = exchange(pair_ref, pair_all, send_first, recv_first)
     pair_all[my_block, :] = pair_ref[...]
 
@@ -405,9 +426,6 @@
     mask_lanes = jnp.sum(jnp.where(key_lane, mask_all, 0.0), axis=0, keepdims=True)
     key_lane_ones = jnp.where(key_lane, 1.0, 0.0)
 
-    for copy in copies_first:
-        copy.wait_recv()
-
     def sides(chunk, normed_rows, weight_ref):
         projected = dot(normed_rows, weight_ref[...])
         rows_mask = mask_wide[pl.ds(chunk * tile, tile), :]
@@ -440,11 +458,15 @@
         rows_normed = norm_rows(start, average)
         normed[rows, :] = rows_normed
         left_side, right_side = sides(chunk, rows_normed, out_project_ref)
-        left[rows, :] = left_side
-        right[rows, :] = right_side
+        for row in range(tile):
+            piece = slice(row * length, (row + 1) * length)
+            turned = pl.ds(chunk * tile + row, length, stride=length)
+            left[turned, :] = left_side[piece, :]
+            right[turned, :] = right_side[piece, :]
         return carry
 
-    lax.fori_loop(0, chunks, first, 0)
+    for order in range(chunks):
+        first(arrivals(pair_all, send_first, recv_first, order), 0)
 
     def finish(rows, combined, gate_ref, final_ref):
         combined_normed = norm_rows(combined.astype(bf16), average)
@@ -453,42 +475,6 @@
         return (current[rows, :].astype(f32) + gate * update).astype(bf16)
 
     def outgoing(chunk, carry):
-        rows = pl.ds(pl.multiple_of(chunk * chunk_rows, chunk_rows), chunk_rows)
-
-        def add(step, totals):
-            totals = list(totals)
-            tiles = [
-                left[pl.ds(pl.multiple_of((chunk * tile + row) * length + step * tile, tile), tile), :]
-                for row in range(tile)
-            ]
-            for offset in range(tile):
-                others = right[pl.ds(step * tile + offset, length, stride=length), :]
-                for row in range(tile):
-                    totals[row] = totals[row] + tiles[row][offset : offset + 1, :] * others
-            return tuple(totals)
-
-        totals = lax.fori_loop(
-            0, chunks, add, tuple(jnp.zeros((length, width), f32) for _ in range(tile))
-        )
-        combined = jnp.concatenate(totals, axis=0)
-        updated = finish(rows, combined, out_gate_ref, out_final_ref)
-        current[rows, :] = updated
-        return carry
-
-    lax.fori_loop(0, chunks, outgoing, 0)
-
-    def second(chunk, carry):
-        rows = pl.ds(pl.multiple_of(chunk * chunk_rows, chunk_rows), chunk_rows)
-        rows_normed = norm_rows(current[rows, :], average)
-        normed[rows, :] = rows_normed
-        left_side, right_side = sides(chunk, rows_normed, in_project_ref)
-        left[rows, :] = left_side
-        right[rows, :] = right_side
-        return carry
-
-    lax.fori_loop(0, chunks, second, 0)
-
-    def incoming(chunk, carry):
         rows = pl.ds(pl.multiple_of(chunk * chunk_rows, chunk_rows), chunk_rows)
 
         def add(step, totals):
@@ -502,7 +488,41 @@
             return tuple(totals)
 
         totals = lax.fori_loop(
-            0, chunks, add, tuple(jnp.zeros((length, width), f32) for _ in range(tile))
+            0, chunks, add, tuple(jnp.zeros((length, width), f32) for _ in range(tile)), unroll=True
+        )
+        combined = jnp.concatenate(totals, axis=0)
+        updated = finish(rows, combined, out_gate_ref, out_final_ref)
+        current[rows, :] = updated
+        return carry
+
+    lax.fori_loop(0, chunks, outgoing, 0, unroll=2)
+
+    def second(chunk, carry):
+        rows = pl.ds(pl.multiple_of(chunk * chunk_rows, chunk_rows), chunk_rows)
+        rows_normed = norm_rows(current[rows, :], average)
+        normed[rows, :] = rows_normed
+        left_side, right_side = sides(chunk, rows_normed, in_project_ref)
+        left[rows, :] = left_side
+        right[rows, :] = right_side
+        return carry
+
+    lax.fori_loop(0, chunks, second, 0, unroll=True)
+
+    def incoming(chunk, carry):
+        rows = pl.ds(pl.multiple_of(chunk * chunk_rows, chunk_rows), chunk_rows)
+
+        def add(step, totals):
+            totals = list(totals)
+            for offset in range(tile):
+                base = (step * tile + offset) * length
+                own = left[pl.ds(pl.multiple_of(base + chunk * tile, tile), tile), :]
+                others = right[pl.ds(pl.multiple_of(base, length), length), :]
+                for row in range(tile):
+                    totals[row] = totals[row] + own[row : row + 1, :] * others
+            return tuple(totals)
+
+        totals = lax.fori_loop(
+            0, chunks, add, tuple(jnp.zeros((length, width), f32) for _ in range(tile)), unroll=True
         )
         combined = jnp.concatenate(totals, axis=0)
         updated = finish(rows, combined, in_gate_ref, in_final_ref)
@@ -525,7 +545,7 @@
         ).astype(f32)
         return carry
 
-    lax.fori_loop(0, chunks, incoming, 0)
+    lax.fori_loop(0, chunks, incoming, 0, unroll=2)
 
     before = current[my_block, :]
     projected = dot(norm_rows(before, average), start_project_ref[...])
@@ -557,8 +577,6 @@
     own = own_rows[...]
     after_start[my_block, :] = own
     own_projected = dot(norm_rows(own, average), end_project_ref[...])
-    for copy in copies_second:
-        copy.wait_recv()
 
     def columns(chunk, carry):
         rows = pl.ds(pl.multiple_of(chunk * chunk_rows, chunk_rows), chunk_rows)
@@ -569,7 +587,8 @@
         left[rows, :] = dot(rows_normed, end_bias_wide).astype(bf16).astype(f32)
         return carry
 
-    lax.fori_loop(0, chunks, columns, 0)
+    for order in range(chunks):
+        columns(arrivals(after_start, send_second, recv_second, order), 0)
     gates = sigmoid(own_projected[:, 3 * width :])
     attended = []
     for row in range(mine):
@@ -594,7 +613,7 @@
                 ] = piece
             return top
 
-        top = lax.fori_loop(0, chunks, score, jnp.full((length, width), -jnp.inf, f32))
+        top = lax.fori_loop(0, chunks, score, jnp.full((length, width), -jnp.inf, f32), unroll=True)
 
         def mix(step, totals):
             total, mixed = totals
@@ -606,7 +625,7 @@
             return total, mixed
 
         zero = jnp.zeros((length, width), f32)
-        total, mixed = lax.fori_loop(0, chunks, mix, (zero, zero))
+        total, mixed = lax.fori_loop(0, chunks, mix, (zero, zero), unroll=True)
         attended.append((mixed / total * gates[slice(row * length, (row + 1) * length), :]).astype(bf16))
     update = dot(jnp.concatenate(attended, axis=0), end_final_ref[...]).astype(bf16)
     after_end = (own.astype(f32) + update.astype(f32)).astype(bf16)
@@ -680,6 +699,9 @@
             heads * length == width
             and width // heads == length
             and mine * devices == length
+            and 8 % mine == 0
+            and length % 8 == 0
+            and (length // 8) & (length // 8 - 1) == 0
             and (mine * length) % 16 == 0
         )
         if fits:

time: 39.7 us -> 34 us (0.86)
  the two profiles are of different devices: /device:TPU:0 before, /device:TPU:17 now
where the time goes in v3:
time: 34 us; the launch traced here: 33.8 us
  Pallas kernels  32.5 us (96%)
  local copies, waits for them, and re-layouts  1.32 us (4%)
    pallas_call x1, Pallas kernels, fused(): pl.pallas_call(functools.partial(fused_kernel, devices, count), out_shape...  32.5 us
    unnamed x1, local copies, waits for them, and re-layouts  1.32 us

profile of v3, /device:TPU:17, one launch (start us, length us, event | category | flops | bytes accessed | tf_op | source)
XLA Modules:
  0.0 33.8 jit_solution(2710805997763195126)
XLA Ops:
  0.0 32.5 %shard_map.172 = bf16[64,128]{1,0:T(8,128)(2,1)} custom-call(bf16[64,128]{1,0:T(8,128)(2,1)} %bitcast.7, s32[1,32]{1,0:T(1,128)} %bitcast.10, s32[1,32]{1,0:T(1,128)} %bitcast.11, f32[2,128]{1,0:T(2,128)} %refs_3_.1, bf16[128,512]{1,0:T(8,128)(2,1)} %refs_4_.1, bf16[128,128]{1,0:T(8,128)(2,1)} %refs_5_.1, bf16[128,128]{1,0:T(8,128)(2,1)} %refs_6_.1, ...), custom_call_target="tpu_custom_call" | custom-call | tf_op jit(solution)/shard_map/pallas_call | solution.py:659
  32.5 1.3 %copy.20 = bf16[2,32,128]{2,1,0:T(8,128)(2,1)} copy(bf16[2,32,128]{2,1,0:T(8,128)(2,1)} %bitcast.6) | data formatting | bytes 32768
